TPU v7x, 512 devices: a whole 4x4x16 slice. The times are simulated.
512 devices in a mesh: row: 32 (over y, x, core), col: 16 (over z).
Axes of the slice: x: 4, y: 4, z: 16, core: 2. Of those that a mesh axis runs over, the one named last changes fastest.
Arguments:
- iterate: float32 [5120, 8192], P('row', 'col'), may hold values from -0.05 to 0.05
Outputs:
- update: float32 [5120, 8192], P('row', 'col')
All inputs are finite; a program needn't handle non-finite values.
Results may differ from a plain program's by a relative error of at most 0.0022.
Values may be sent and summed in bfloat16 or wider, within the bound.
A program may use at most 64 MiB of HBM per device.

v0:
```python
import math

import jax
import jax.numpy as jnp
from jax import lax
from jax.sharding import PartitionSpec as P

coef_a = 3.4445
coef_b = -4.775
coef_c = 2.0315


def local(iterate):
    iter_b = iterate.astype(jnp.bfloat16)
    slab = lax.all_gather(iter_b, "row", axis=0, tiled=True)
    partial_value = lax.dot_general(
        iter_b, slab, (((1,), (1,)), ((), ())), preferred_element_type=jnp.float32
    )
    gram = lax.psum_scatter(partial_value, "col", scatter_dimension=1, tiled=True)
    gram_b = gram.astype(jnp.bfloat16)
    row_panel = lax.all_gather(gram_b, "col", axis=1, tiled=True)
    square = jnp.dot(
        row_panel,
        lax.all_gather(gram_b, "row", axis=0, tiled=True),
        preferred_element_type=jnp.float32,
    )
    mixed = (coef_b * gram + coef_c * square).astype(jnp.bfloat16)
    product = jnp.dot(
        lax.all_gather(mixed, "col", axis=1, tiled=True), slab, preferred_element_type=jnp.float32
    )
    columns_all = iterate.shape[1] * lax.axis_size("col")
    return 0.2 * math.sqrt(columns_all) * (coef_a * iterate + product)


def solution(mesh):
    return jax.shard_map(
        local,
        mesh=mesh,
        in_specs=(P("row", "col"),),
        out_specs=P("row", "col"),
        check_vma=False,
    )
```

profile of v0, /device:TPU:6, one launch (start us, length us, event | category | flops | bytes accessed | tf_op | source)
XLA Modules:
  0.0 394.1 jit_solution(9006903878256888706)
XLA Ops:
  6.5 0.0 all-gather.7.cloned.1.call-start
  6.5 1.7 convert_element_type.9
  8.2 0.0 all-gather.7.cloned.1.call-update
  8.2 0.0 reduce-scatter.4.cloned.1.call-start
  8.3 69.0 %all-gather.7.cloned.1.call-done = bf16[5120,512]{1,0:T(8,128)(2,1)} async-done(((bf16[160,512]{1,0:T(8,128)(2,1)}), bf16[5120,512]{1,0:T(8,128)(2,1)}) %all-gather.7.cloned.1.call-update) | async-done | bytes 5242896 | tf_op jit(solution)/shard_map/all_gather | solution.py:15
  77.3 6.5 %convolution_bitcast_fusion = f32[5120,160]{1,0:T(8,128)} fusion(bf16[160,512]{1,0:T(8,128)(2,1)} %convert_element_type.9, bf16[5120,512]{1,0:T(8,128)(2,1)} %all-gather.7.cloned.1.call-done), kind=kOutput, calls=%fused_computation | convolution fusion | flops 838860800 | bytes 8683520
  83.7 0.0 reduce-scatter.4.cloned.1.call-update
  83.8 0.0 all-gather.11.cloned.1.call-start
  83.8 82.9 %reduce-scatter.4.cloned.1.call-done = f32[320,160]{1,0:T(8,128)} async-done(((f32[5120,160]{1,0:T(8,128)}), f32[320,160]{1,0:T(8,128)}) %reduce-scatter.4.cloned.1.call-update) | async-done | bytes 204816
  166.7 1.1 copy.7
  167.8 0.7 convert_bitcast_fusion
  168.5 0.0 all-gather.11.cloned.1.call-update
  168.5 0.0 all-gather.9.cloned.1.call-start
  168.5 0.7 convert_element_type.10
  169.2 0.0 all-gather.9.cloned.1.call-update
  169.2 0.0 all-gather.13.cloned.1.call-start
  169.3 70.9 %all-gather.11.cloned.1.call-done = bf16[16,320,160]{1,2,0:T(8,128)(2,1)} async-done(((bf16[1,320,160]{1,2,0:T(8,128)(2,1)}), bf16[16,320,160]{1,2,0:T(8,128)(2,1)}) %all-gather.11.cloned.1.call-update) | async-done | bytes 1638416 | tf_op jit(solution)/shard_map/all_gather | solution.py:21
  240.1 2.2 copy.4
  242.4 2.5 reshape.1
  244.9 55.7 %all-gather.9.cloned.1.call-done = bf16[5120,320]{1,0:T(8,128)(2,1)} async-done(((bf16[160,320]{1,0:T(8,128)(2,1)}), bf16[5120,320]{1,0:T(8,128)(2,1)}) %all-gather.9.cloned.1.call-update) | async-done | bytes 3276816 | tf_op jit(solution)/shard_map/all_gather | solution.py:24
  300.6 4.3 %fusion.3 = bf16[1,320,160]{1,2,0:T(8,128)(2,1)} fusion(bf16[5120,160]{0,1:T(8,128)(2,1)} %reshape.1, bf16[5120,320]{1,0:T(8,128)(2,1)} %all-gather.9.cloned.1.call-done, f32[160,320]{1,0:T(8,128)S(1)} %copy.7), kind=kOutput, calls=%fused_computation.6 | convolution fusion | flops 524492800 | bytes 5222400 | tf_op jit(solution)/shard_map/dot_general | solution.py:22
  304.9 0.0 copy-start
  304.9 0.0 all-gather.13.cloned.1.call-update
  304.9 73.1 %all-gather.13.cloned.1.call-done = bf16[16,320,160]{1,2,0:T(8,128)(2,1)} async-done(((bf16[1,320,160]{1,2,0:T(8,128)(2,1)}), bf16[16,320,160]{1,2,0:T(8,128)(2,1)}) %all-gather.13.cloned.1.call-update) | async-done | bytes 1638416 | tf_op jit(solution)/shard_map/all_gather | solution.py:29
  378.0 2.2 copy.5
  380.3 2.5 reshape.3
  382.8 0.0 copy-done
  382.8 4.7 %fusion = f32[160,512]{1,0:T(8,128)} fusion(bf16[5120,160]{0,1:T(8,128)(2,1)} %reshape.3, bf16[5120,512]{1,0:T(8,128)(2,1)} %all-gather.7.cloned.1.call-done, f32[160,512]{1,0:T(8,128)S(1)} %copy-done), kind=kOutput, calls=%fused_computation.2 | convolution fusion | flops 839106560 | bytes 7536640 | tf_op jit(solution)/shard_map/dot_general | solution.py:28
Async XLA Ops:
  6.5 70.8 %all-gather.7.cloned.1.call-start = ((), (), s32[]{:S(2)}) async-start(), calls=%async_computation.1 | async-start | bytes 5406720 | tf_op jit(solution)/shard_map/all_gather | solution.py:15
  8.2 158.5 %reduce-scatter.4.cloned.1.call-start = ((), (), s32[]{:S(2)}) async-start(), calls=%async_computation.5 | async-start | bytes 5570560
  83.8 156.4 %all-gather.11.cloned.1.call-start = ((), (), s32[]{:S(2)}) async-start(), calls=%async_computation.3 | async-start | bytes 2088960 | tf_op jit(solution)/shard_map/all_gather | solution.py:21
  168.5 132.1 %all-gather.9.cloned.1.call-start = ((), (), s32[]{:S(2)}) async-start(), calls=%async_computation.2 | async-start | bytes 4055040 | tf_op jit(solution)/shard_map/all_gather | solution.py:24
  169.2 208.8 %all-gather.13.cloned.1.call-start = ((), (), s32[]{:S(2)}) async-start(), calls=%async_computation.4 | async-start | bytes 2088960 | tf_op jit(solution)/shard_map/all_gather | solution.py:29
  304.9 77.9 %copy-start = (f32[160,512]{1,0:T(8,128)S(1)}, f32[160,512]{1,0:T(8,128)}, u32[]{:S(2)}) copy-start(f32[160,512]{1,0:T(8,128)} %param.1) | copy-start | bytes 983044
Sparse Core Ops, SparseCore 0:
  10.5 66.7 all-gather.6
  83.9 82.7 reduce-scatter.3
  168.8 71.3 all-gather.10
  243.1 57.4 all-gather.8
  305.0 72.9 all-gather.12
where the time goes:
time: 394 us
  waiting for transfers between devices  352 us (89%)
  matrix products  15.5 us (4%)
  between operations  13.2 us (3%)
  local copies, waits for them, and re-layouts  10.7 us (3%)
    unnamed x6, waiting for transfers between devices  82.9 us
    all_gather x1, waiting for transfers between devices, local(): lax.all_gather(mixed, 'col', axis=1, tiled=True)  73.1 us
    all_gather x1, waiting for transfers between devices, local(): row_panel = lax.all_gather(gram_b, 'col', axis=1, tiled=True)  70.9 us
    all_gather x1, waiting for transfers between devices, local(): slab = lax.all_gather(iter_b, 'row', axis=0, tiled=True)  69 us
    all_gather x1, waiting for transfers between devices, local(): lax.all_gather(gram_b, 'row', axis=0, tiled=True)  55.7 us
  transfers between devices with their start and end apart: 5, of which 5 were waited for; matrix products, arithmetic and copies ran while one was open for 1% of the time, Pallas kernels for 0%

commit v1 on v0

v1 whole, which is shorter than its diff:
```python
import functools
import math

import jax
import jax.numpy as jnp
from jax import lax
from jax.experimental import pallas as pl
from jax.experimental.pallas import tpu as pltpu
from jax.sharding import PartitionSpec as P

coef_a = 3.4445
coef_b = -4.775
coef_c = 2.0315

NX = 4
NY = 4
NZ = 16
BLOCK = 160
HALF = 80
WIDE = 640
COLS = 512
SUBS = 2
MESH = pl.DeviceIdType.MESH


class Copies:
    def __init__(self):
        self.started = []

    def start(self, src, dst, send_sem, recv_sem, device):
        copy = pltpu.make_async_remote_copy(
            src_ref=src,
            dst_ref=dst,
            send_sem=send_sem,
            recv_sem=recv_sem,
            device_id=device,
            device_id_type=MESH,
        )
        copy.start()
        self.started.append(copy)

    def finish(self):
        for copy in self.started:
            copy.wait_send()


def arrived(ref, send_sem, recv_sem, device):
    pltpu.make_async_remote_copy(
        src_ref=ref,
        dst_ref=ref,
        send_sem=send_sem,
        recv_sem=recv_sem,
        device_id=device,
        device_id_type=MESH,
    ).wait_recv()


class PlaneGather:
    def __init__(self, copies, way, place, view, cut, total, send, recv):
        self.copies, self.way, self.place, self.view = copies, way, place, view
        self.cuts = ((0, cut), (cut, total - cut))
        self.send, self.recv = send, recv

    def coords(self, a, b):
        x, y, _, _ = self.place
        dx, dy = (a, b) if self.way == 0 else (b, a)
        return lax.rem(x + (dx % 4), 4), lax.rem(y + (dy % 4), 4)

    def block(self, a, b, core=None):
        x, y = self.coords(a, b)
        core = self.place[2] if core is None else core
        return core * 16 + y * 4 + x

    def device(self, a, b):
        x, y = self.coords(a, b)
        return {"row": (y * 4 + x) * 2 + self.place[2], "col": self.place[3]}

    def sibling(self):
        x, y, core, z = self.place
        return {"row": (y * 4 + x) * 2 + 1 - core, "col": z}

    def half(self, index, part):
        start, size = self.cuts[part]
        return self.view(index).at[pl.ds(start, size), :]

    def push(self, a, b, to, slot, part=None):
        index = self.block(a, b)
        ref = self.view(index) if part is None else self.half(index, part)
        device = self.sibling() if to is None else self.device(*to)
        self.copies.start(ref, ref, self.send.at[slot], self.recv.at[slot], device)

    def wait(self, a, b, slot, part=None, core=None):
        index = self.block(a, b, core)
        ref = self.view(index) if part is None else self.half(index, part)
        arrived(ref, self.send.at[slot], self.recv.at[slot], self.sibling())

    def second(self, a):
        k = a % 4
        self.push(a, 0, (0, 1), 4 + 2 * k)
        self.push(a, 0, (0, -1), 5 + 2 * k)

    def other(self, a, b):
        self.push(a, b, None, 20 + (a % 4) * 4 + b % 4)

    def own(self):
        self.push(0, 0, (1, 0), 0)
        self.push(0, 0, (-1, 0), 1)
        self.second(0)
        self.other(0, 0)

    def first(self):
        self.wait(-1, 0, 0)
        self.push(-1, 0, (1, 0), 2, part=0)
        self.second(-1)
        self.wait(1, 0, 1)
        self.push(1, 0, (-1, 0), 3, part=1)
        self.second(1)
        self.other(-1, 0)
        self.other(1, 0)

    def first_far(self):
        self.wait(2, 0, 2, part=0)
        self.wait(2, 0, 3, part=1)
        self.second(2)
        self.other(2, 0)

    def then(self, a):
        k = a % 4
        self.wait(a, -1, 4 + 2 * k)
        self.push(a, -1, (0, 1), 12 + 2 * k, part=0)
        self.wait(a, 1, 5 + 2 * k)
        self.push(a, 1, (0, -1), 13 + 2 * k, part=1)
        self.other(a, -1)
        self.other(a, 1)

    def then_far(self, a):
        k = a % 4
        self.wait(a, 2, 12 + 2 * k, part=0)
        self.wait(a, 2, 13 + 2 * k, part=1)
        self.other(a, 2)

    def others(self):
        for a in range(4):
            for b in range(4):
                self.wait(a, b, 20 + a * 4 + b, core=1 - self.place[2])


class RingGather:
    def __init__(self, copies, buf, place, up, down, send, recv):
        self.copies, self.buf, self.z = copies, buf, place[3]
        self.up, self.down, self.send, self.recv = up, down, send, recv

    def plane(self, d):
        return lax.rem(self.z + d % NZ, NZ)

    def step(self, s):
        if s > 1:
            self.wait_up(s - 1)
        ref = self.buf.at[self.plane(1 - s)]
        self.copies.start(ref, ref, self.send.at[0, s], self.recv.at[0, s], self.up)
        if s <= 7:
            if s > 1:
                self.wait_down(s - 1)
            ref = self.buf.at[self.plane(s - 1)]
            self.copies.start(ref, ref, self.send.at[1, s], self.recv.at[1, s], self.down)

    def wait_up(self, s):
        arrived(self.buf.at[self.plane(-s)], self.send.at[0, s], self.recv.at[0, s], self.up)

    def wait_down(self, s):
        arrived(self.buf.at[self.plane(s)], self.send.at[1, s], self.recv.at[1, s], self.down)


def kernel(
    x_ref, out_ref,
    slab, cw, ccw, gram, grow, gcol, mrow,
    xs, xr, rs_s, rs_r, gs, gr, cs, cr, ms, mr,
):
    row, z = lax.axis_index("row"), lax.axis_index("col")
    core = lax.rem(row, 2)
    x = lax.rem(row // 2, 4)
    y = row // 8
    zh, zl = z // 2, lax.rem(z, 2)
    place = (x, y, core, z)
    me = core * 16 + y * 4 + x
    up = {"row": row, "col": lax.rem(z + 1, NZ)}
    down = {"row": row, "col": lax.rem(z + NZ - 1, NZ)}

    copies = Copies()
    gather_x = [
        PlaneGather(
            copies, w, place, lambda i, w=w: slab.at[w, i], 80, BLOCK, xs.at[w], xr.at[w]
        )
        for w in range(2)
    ]

    barrier = pltpu.get_barrier_semaphore()
    g0 = gather_x[0]
    for device in (
        g0.device(1, 0), g0.device(-1, 0), g0.device(0, 1), g0.device(0, -1), g0.sibling(), up, down,
    ):
        pl.semaphore_signal(barrier, inc=1, device_id=device, device_id_type=MESH)
    slab[0, me] = x_ref[:, 0:256].astype(jnp.bfloat16)
    slab[1, me] = x_ref[:, 256:512].astype(jnp.bfloat16)
    pl.semaphore_wait(barrier, 7)

    for g in gather_x:
        g.own()
    for g in gather_x:
        g.first()
    for g in gather_x:
        g.first_far()
    for a in (0, -1, 1, 2):
        for g in gather_x:
            g.then(a)
    for a in (0, -1, 1, 2):
        for g in gather_x:
            g.then_far(a)
    for g in gather_x:
        g.others()

    def share(d):
        dh, dl = d // 2, lax.rem(d, 2)
        value = None
        for h in range(2):
            left = slab[h, me, pl.ds(pl.multiple_of(dl * HALF, 16), HALF), :]
            right = slab[h, pl.ds(dh * 4, 4)].reshape(WIDE, 256)
            term = lax.dot_general(
                left, right, (((1,), (1,)), ((), ())), preferred_element_type=jnp.float32
            )
            value = term if value is None else value + term
        return value

    rows = HALF // SUBS

    def piece(buf, slot, j):
        return buf.at[slot, pl.ds(j * rows, rows), :]

    def ring_copy(way, buf, slot, j, device):
        return pltpu.make_async_remote_copy(
            src_ref=piece(buf, slot, j),
            dst_ref=piece(buf, slot + 1, j),
            send_sem=rs_s.at[way, slot, j],
            recv_sem=rs_r.at[way, slot + 1, j],
            device_id=device,
            device_id_type=MESH,
        )

    def ring_arrived(way, buf, slot, j):
        arrived(piece(buf, slot, j), rs_s.at[way, slot, j], rs_r.at[way, slot, j], up)

    def ring_step(ways, slot):
        for way in ways:
            buf, device = (cw, up) if way == 0 else (ccw, down)
            d = lax.rem(z + 8 - slot, NZ) if way == 0 else lax.rem(z + 9 + slot, NZ)
            part = share(d)
            for j in range(SUBS):
                ring_arrived(way, buf, slot, j)
                buf[slot, j * rows : (j + 1) * rows, :] += part[j * rows : (j + 1) * rows]
                ring_copy(way, buf, slot, j, device).start()

    for way, buf, device, d in ((0, cw, up, z + 8), (1, ccw, down, z + 9)):
        buf[0] = share(lax.rem(d, NZ))
        for j in range(SUBS):
            ring_copy(way, buf, 0, j, device).start()

    @pl.loop(1, 7)
    def _(slot):
        ring_step((0, 1), slot)

    ring_step((0,), 7)
    gram[...] = share(z)
    for j in range(SUBS):
        ring_arrived(1, ccw, 7, j)
        ring_arrived(0, cw, 8, j)
    gram[...] += cw[8] + ccw[7]

    gather_g = RingGather(copies, grow, place, up, down, gs, gr)
    gather_c = [
        PlaneGather(
            copies, w, place, lambda i, half=half: gcol.at[i, half], 48, HALF, cs.at[w], cr.at[w]
        )
        for w, half in ((0, zl), (1, 1 - zl))
    ]
    gb = gram[...].astype(jnp.bfloat16)
    grow[z] = gb
    gcol[me, zl] = gb
    gather_g.step(1)
    gather_c[0].own()
    gather_g.step(2)

    mate = jnp.where(zl == 0, 1, NZ - 1)
    gcol[me, 1 - zl] = grow[lax.rem(z + mate, NZ)]
    gather_c[1].own()
    gather_c[0].first()
    gather_g.step(3)
    gather_c[1].first()
    gather_c[0].first_far()
    gather_c[1].first_far()
    gather_g.step(4)
    for i, a in enumerate((0, -1, 1, 2)):
        for g in gather_c:
            g.then(a)
        gather_g.step(5 + i)
    for a in (0, -1, 1, 2):
        for g in gather_c:
            g.then_far(a)
    for g in gather_c:
        g.others()
    gather_g.wait_up(8)
    gather_g.wait_down(7)

    def square_step(i, total):
        return total + jnp.dot(
            grow[2 * i + zl],
            gcol[pl.ds(4 * i, 4)].reshape(WIDE, WIDE),
            preferred_element_type=jnp.float32,
        )

    square = lax.fori_loop(0, 8, square_step, jnp.zeros((HALF, WIDE), jnp.float32))
    mrow[z] = (coef_b * gram[...] + coef_c * square).astype(jnp.bfloat16)

    gather_m = RingGather(copies, mrow, place, up, down, ms, mr)
    for s in range(1, 9):
        gather_m.step(s)
    gather_m.wait_up(8)
    gather_m.wait_down(7)

    scale = 0.2 * math.sqrt(COLS * NZ)
    out_ref[...] = coef_a * x_ref[...]

    @pl.loop(0, 8)
    def _(i):
        left = mrow[pl.ds(2 * i, 2)].reshape(BLOCK, WIDE)
        for h in range(2):
            right = slab[h, pl.ds(4 * i, 4)].reshape(WIDE, 256)
            out_ref[:, h * 256 : (h + 1) * 256] += jnp.dot(
                left, right, preferred_element_type=jnp.float32
            )

    out_ref[...] = scale * out_ref[...]

    copies.finish()

    for j in range(SUBS):

        @pl.loop(0, 7)
        def _(slot):
            ring_copy(0, cw, slot, j, up).wait_send()
            ring_copy(1, ccw, slot, j, down).wait_send()

        ring_copy(0, cw, 7, j, up).wait_send()


def local(iterate):
    dma = pltpu.SemaphoreType.DMA
    return pl.pallas_call(
        kernel,
        out_shape=jax.ShapeDtypeStruct((BLOCK, COLS), jnp.float32),
        in_specs=[pl.BlockSpec(memory_space=pltpu.VMEM)],
        out_specs=pl.BlockSpec(memory_space=pltpu.VMEM),
        scratch_shapes=[
            pltpu.VMEM((2, 32, BLOCK, 256), jnp.bfloat16),
            pltpu.VMEM((9, HALF, WIDE), jnp.float32),
            pltpu.VMEM((8, HALF, WIDE), jnp.float32),
            pltpu.VMEM((HALF, WIDE), jnp.float32),
            pltpu.VMEM((NZ, HALF, WIDE), jnp.bfloat16),
            pltpu.VMEM((32, 2, HALF, WIDE), jnp.bfloat16),
            pltpu.VMEM((NZ, HALF, WIDE), jnp.bfloat16),
            dma((2, 36)),
            dma((2, 36)),
            dma((2, 9, SUBS)),
            dma((2, 9, SUBS)),
            dma((2, 9)),
            dma((2, 9)),
            dma((2, 36)),
            dma((2, 36)),
            dma((2, 9)),
            dma((2, 9)),
        ],
        compiler_params=pltpu.CompilerParams(
            collective_id=0, has_side_effects=True, vmem_limit_bytes=48 * 1024 * 1024
        ),
        cost_estimate=pl.CostEstimate(
            flops=2300000000, bytes_accessed=700000, transcendentals=0
        ),
    )(iterate)


def solution(mesh):
    return jax.shard_map(
        local,
        mesh=mesh,
        in_specs=(P("row", "col"),),
        out_specs=P("row", "col"),
        check_vma=False,
    )
```

time: 394 us -> 151 us (0.38)
  waiting for transfers between devices: 352 us -> 0 us
  Pallas kernels: 0 us -> 149 us
  matrix products: 15.5 us -> 0 us
  between operations: 13.2 us -> 0.01 us
  local copies, waits for them, and re-layouts: 10.7 us -> 1.7 us
    all_gather x4 -> x0, waiting for transfers between devices: 269 us -> none  [the longest x1 73.1 us: local(): lax.all_gather(mixed, 'col', axis=1, tiled=True)]
    pallas_call x0 -> x1, Pallas kernels: none -> 149 us  [local(): pl.pallas_call(kernel, out_shape=jax.ShapeDtypeStruct((BLOCK, COLS), jnp....]
    unnamed x6 -> x0, waiting for transfers between devices: 82.9 us -> none
    dot_general x2 -> x0, matrix products: 9.02 us -> none  [the longest x1 4.74 us: local(): jnp.dot(lax.all_gather(mixed, 'col', axis=1, tiled=True), slab, preferred...]
    unnamed x1 -> x0, matrix products: 6.45 us -> none
    unnamed x5 -> x3, local copies, waits for them, and re-layouts: 6.18 us -> 1.7 us
    all_gather x2 -> x0, local copies, waits for them, and re-layouts: 4.47 us -> none  [the longest x1 2.23 us: local(): lax.all_gather(mixed, 'col', axis=1, tiled=True)]
  transfers between devices with their start and end apart: 5 -> 0, of which waited for: 5 -> 0; matrix products, arithmetic and copies ran while one was open for 1% -> 0% of each run, Pallas kernels for 0% -> 0%
where the time goes in v1:
time: 151 us
  Pallas kernels  149 us (99%)
  local copies, waits for them, and re-layouts  1.7 us (1%)
    pallas_call x1, Pallas kernels, local(): pl.pallas_call(kernel, out_shape=jax.ShapeDtypeStruct((BLOCK, COLS), jnp....  149 us

profile of v1, /device:TPU:6, one launch (start us, length us, event | category | flops | bytes accessed | tf_op | source)
XLA Modules:
  0.0 151.2 jit_solution(13452362491753095883)
XLA Ops:
  0.0 0.0 copy-start
  0.0 1.0 copy-done
  1.0 149.5 %shard_map.17 = f32[160,512]{1,0:T(8,128)S(1)} custom-call(f32[160,512]{1,0:T(8,128)S(1)} %copy-done), custom_call_target="tpu_custom_call" | custom-call | flops 2300000000 | bytes 700000 | tf_op jit(solution)/shard_map/pallas_call | solution.py:357
  150.4 0.7 copy.3
Async XLA Ops:
  0.0 1.0 copy-start

commit v2 on v1

v2 whole, which is shorter than its diff:
```python
import functools
import math

import jax
import jax.numpy as jnp
from jax import lax
from jax.experimental import pallas as pl
from jax.experimental.pallas import tpu as pltpu
from jax.sharding import PartitionSpec as P

coef_a = 3.4445
coef_b = -4.775
coef_c = 2.0315

NX = 4
NY = 4
NZ = 16
BLOCK = 160
HALF = 80
WIDE = 640
COLS = 512
SUBS = 2
PIECES = 5
MESH = pl.DeviceIdType.MESH


def remote(ref, send_sem, recv_sem, device):
    return pltpu.make_async_remote_copy(
        src_ref=ref,
        dst_ref=ref,
        send_sem=send_sem,
        recv_sem=recv_sem,
        device_id=device,
        device_id_type=MESH,
    )


class PlaneGather:
    def __init__(self, way, place, view, cut, total, send, recv):
        self.way, self.place, self.view = way, place, view
        self.cuts = ((0, cut), (cut, total - cut))
        self.send, self.recv = send, recv

    def coords(self, a, b):
        x, y, _, _ = self.place
        dx, dy = (a, b) if self.way == 0 else (b, a)
        return lax.rem(x + (dx % 4), 4), lax.rem(y + (dy % 4), 4)

    def block(self, a, b, core=None):
        x, y = self.coords(a, b)
        core = self.place[2] if core is None else core
        return core * 16 + y * 4 + x

    def device(self, a, b):
        x, y = self.coords(a, b)
        return {"row": (y * 4 + x) * 2 + self.place[2], "col": self.place[3]}

    def sibling(self):
        x, y, core, z = self.place
        return {"row": (y * 4 + x) * 2 + 1 - core, "col": z}

    def half(self, index, part):
        start, size = self.cuts[part]
        return self.view(index).at[pl.ds(start, size), :]

    def push(self, a, b, to, slot, part=None):
        index = self.block(a, b)
        ref = self.view(index) if part is None else self.half(index, part)
        device = self.sibling() if to is None else self.device(*to)
        remote(ref, self.send, self.recv.at[slot], device).start()

    def wait(self, a, b, slot, part=None, core=None):
        index = self.block(a, b, core)
        ref = self.view(index) if part is None else self.half(index, part)
        remote(ref, self.send, self.recv.at[slot], self.sibling()).wait_recv()

    def second(self, a):
        k = a % 4
        self.push(a, 0, (0, 1), 4 + 2 * k)
        self.push(a, 0, (0, -1), 5 + 2 * k)

    def other(self, a, b):
        self.push(a, b, None, 20)

    def own(self):
        self.push(0, 0, (1, 0), 0)
        self.push(0, 0, (-1, 0), 1)
        self.second(0)
        self.other(0, 0)

    def first(self):
        self.wait(-1, 0, 0)
        self.push(-1, 0, (1, 0), 2, part=0)
        self.second(-1)
        self.wait(1, 0, 1)
        self.push(1, 0, (-1, 0), 3, part=1)
        self.second(1)
        self.other(-1, 0)
        self.other(1, 0)

    def first_far(self):
        self.wait(2, 0, 2, part=0)
        self.wait(2, 0, 3, part=1)
        self.second(2)
        self.other(2, 0)

    def then(self, a):
        k = a % 4
        self.wait(a, -1, 4 + 2 * k)
        self.push(a, -1, (0, 1), 12 + 2 * k, part=0)
        self.wait(a, 1, 5 + 2 * k)
        self.push(a, 1, (0, -1), 13 + 2 * k, part=1)
        self.other(a, -1)
        self.other(a, 1)

    def then_far(self, a):
        k = a % 4
        self.wait(a, 2, 12 + 2 * k, part=0)
        self.wait(a, 2, 13 + 2 * k, part=1)
        self.other(a, 2)

    def others(self, blocks):
        remote(blocks, self.send, self.recv.at[20], self.sibling()).wait_recv()


class RingGather:
    def __init__(self, buf, place, stride, send, recv):
        self.buf, self.stride, self.send, self.recv = buf, stride, send, recv
        self.row, self.z = (place[1] * 4 + place[0]) * 2 + place[2], place[3]
        self.far = NZ // stride // 2

    def plane(self, d):
        return lax.rem(self.z + d * self.stride + 2 * NZ, NZ)

    def copy(self, way, s, j):
        ref = self.buf.at[self.plane(1 - s if way == 0 else s - 1) // self.stride, pl.ds(j * 16, 16), :]
        device = {"row": self.row, "col": self.plane(1 if way == 0 else -1)}
        return remote(ref, self.send, self.recv.at[way, s, j], device)

    def wait(self, way, s, j):
        ref = self.buf.at[self.plane(-s if way == 0 else s) // self.stride, pl.ds(j * 16, 16), :]
        device = {"row": self.row, "col": self.plane(1)}
        remote(ref, self.send, self.recv.at[way, s, j], device).wait_recv()

    def pieces(self, last):
        for j in range(PIECES):
            for way in range(2):
                if not last or (way == 0) == (j < 3):
                    yield way, j

    def step(self, s, first=False, last=False):
        for way, j in self.pieces(last):
            if not first:
                self.wait(way, s - 1, j)
            self.copy(way, s, j).start()
        if last:
            for way, j in self.pieces(False):
                if (way == 0) != (j < 3):
                    self.wait(way, s - 1, j)

    def end(self):
        for way, j in self.pieces(True):
            self.wait(way, self.far, j)


def kernel(
    x_ref, out_ref,
    slab, cw, ccw, gram, grow, gcol, mrow,
    sent, xr, rs_r, gr, cr, mr,
):
    row, z = lax.axis_index("row"), lax.axis_index("col")
    core = lax.rem(row, 2)
    x = lax.rem(row // 2, 4)
    y = row // 8
    zh, zl = z // 2, lax.rem(z, 2)
    place = (x, y, core, z)
    me = core * 16 + y * 4 + x
    up = {"row": row, "col": lax.rem(z + 1, NZ)}
    down = {"row": row, "col": lax.rem(z + NZ - 1, NZ)}

    gather_x = [
        PlaneGather(
            w, place, lambda i, w=w: slab.at[w, i], 80, BLOCK, sent.at[0], xr.at[w]
        )
        for w in range(2)
    ]

    barrier = pltpu.get_barrier_semaphore()
    g0 = gather_x[0]
    for device in (
        g0.device(1, 0), g0.device(-1, 0), g0.device(0, 1), g0.device(0, -1), g0.sibling(), up, down,
    ):
        pl.semaphore_signal(barrier, inc=1, device_id=device, device_id_type=MESH)
    slab[0, me] = x_ref[:, 0:256].astype(jnp.bfloat16)
    slab[1, me] = x_ref[:, 256:512].astype(jnp.bfloat16)
    pl.semaphore_wait(barrier, 7)

    for g in gather_x:
        g.own()
    for g in gather_x:
        g.first()
    for g in gather_x:
        g.then(0)
    for g in gather_x:
        g.first_far()
    for a in (-1, 1, 2):
        for g in gather_x:
            g.then(a)
    for a in (0, -1, 1, 2):
        for g in gather_x:
            g.then_far(a)
    theirs = pl.ds((1 - core) * 16, 16)
    for g in gather_x:
        g.others(slab.at[g.way, theirs])

    def share(d):
        dh, dl = d // 2, lax.rem(d, 2)
        value = None
        for h in range(2):
            left = slab[h, me, pl.ds(pl.multiple_of(dl * HALF, 16), HALF), :]
            right = slab[h, pl.ds(dh * 4, 4)].reshape(WIDE, 256)
            term = lax.dot_general(
                left, right, (((1,), (1,)), ((), ())), preferred_element_type=jnp.float32
            )
            value = term if value is None else value + term
        return value

    rows = HALF // SUBS

    def piece(buf, slot, j):
        return buf.at[slot, pl.ds(j * rows, rows), :]

    def ring_copy(way, buf, slot, j, device):
        return pltpu.make_async_remote_copy(
            src_ref=piece(buf, slot, j),
            dst_ref=piece(buf, slot + 1, j),
            send_sem=sent.at[1 + way],
            recv_sem=rs_r.at[way, slot + 1, j],
            device_id=device,
            device_id_type=MESH,
        )

    def ring_arrived(way, buf, slot, j):
        remote(piece(buf, slot, j), sent.at[1 + way], rs_r.at[way, slot, j], up).wait_recv()

    def ring_step(ways, slot):
        for way in ways:
            buf, device = (cw, up) if way == 0 else (ccw, down)
            d = lax.rem(z + 8 - slot, NZ) if way == 0 else lax.rem(z + 9 + slot, NZ)
            part = share(d)
            for j in range(SUBS):
                ring_arrived(way, buf, slot, j)
                buf[slot, j * rows : (j + 1) * rows, :] += part[j * rows : (j + 1) * rows]
                ring_copy(way, buf, slot, j, device).start()

    for way, buf, device, d in ((0, cw, up, z + 8), (1, ccw, down, z + 9)):
        buf[0] = share(lax.rem(d, NZ))
        for j in range(SUBS):
            ring_copy(way, buf, 0, j, device).start()

    @pl.loop(1, 7)
    def _(slot):
        ring_step((0, 1), slot)

    ring_step((0,), 7)
    gram[...] = share(z)
    for j in range(SUBS):
        ring_arrived(1, ccw, 7, j)
        ring_arrived(0, cw, 8, j)
    gram[...] += cw[8] + ccw[7]

    gather_g = RingGather(grow, place, 2, sent.at[4], gr)
    gather_c = [
        PlaneGather(
            w, place, lambda i, half=half: gcol.at[i, half], 48, HALF, sent.at[3], cr.at[w]
        )
        for w, half in ((0, zl), (1, 1 - zl))
    ]
    gb = gram[...].astype(jnp.bfloat16)
    gcol[me, zl] = gb
    grow[zh] = gb
    mate = {"row": row, "col": z + 1 - 2 * zl}
    remote(gcol.at[me, zl], sent.at[6], cr.at[0, 21], mate).start()
    gather_c[0].own()
    gather_g.step(1, first=True)
    remote(gcol.at[me, 1 - zl], sent.at[3], cr.at[0, 21], mate).wait_recv()
    gather_c[1].own()
    gather_c[0].first()
    gather_c[0].then(0)
    gather_g.step(2)
    gather_c[1].first()
    gather_c[1].then(0)
    gather_c[0].first_far()
    gather_g.step(3)
    gather_c[0].then(-1)
    gather_c[0].then(1)
    gather_c[1].first_far()
    gather_c[1].then(-1)
    gather_g.step(4, last=True)
    gather_c[1].then(1)
    for g in gather_c:
        g.then(2)
    for a in (0, -1, 1, 2):
        for g in gather_c:
            g.then_far(a)
    gather_c[0].others(gcol.at[theirs, zl])
    gather_c[1].others(gcol.at[theirs, 1 - zl])
    gather_g.end()

    def square_step(i, total):
        return total + jnp.dot(
            grow[i],
            gcol[pl.ds(4 * i, 4)].reshape(WIDE, WIDE),
            preferred_element_type=jnp.float32,
        )

    square = lax.fori_loop(0, 8, square_step, jnp.zeros((HALF, WIDE), jnp.float32))
    mrow[z] = (coef_b * gram[...] + coef_c * square).astype(jnp.bfloat16)

    def product(d):
        q = lax.rem(z + d + NZ, NZ)
        rows_q = pl.ds(pl.multiple_of(lax.rem(q, 2) * HALF, 16), HALF)
        for h in range(2):
            right = slab[h, pl.ds(q // 2 * 4, 4)].reshape(WIDE, 256)
            out_ref[rows_q, h * 256 : (h + 1) * 256] += jnp.dot(
                mrow[q], right, preferred_element_type=jnp.float32
            )

    gather_m = RingGather(mrow, place, 1, sent.at[5], mr)
    gather_m.step(1, first=True)
    out_ref[...] = coef_a * x_ref[...]
    product(0)

    @pl.loop(2, 8)
    def _(s):
        gather_m.step(s)
        product(1 - s)
        product(s - 1)

    gather_m.step(8, last=True)
    product(-7)
    product(7)
    gather_m.end()
    product(8)
    out_ref[...] = (0.2 * math.sqrt(COLS * NZ)) * out_ref[...]

    for k, ref in (
        (0, slab.at[:, pl.ds(0, 31)]),
        (1, cw.at[pl.ds(0, 8)]),
        (2, ccw.at[pl.ds(0, 7)]),
        (3, gcol.at[pl.ds(0, 31)]),
        (6, gcol.at[31, 0]),
        (4, grow.at[pl.ds(0, 7)]),
        (5, mrow.at[pl.ds(0, 15)]),
    ):
        remote(ref, sent.at[k], sent.at[k], up).wait_send()


def local(iterate):
    dma = pltpu.SemaphoreType.DMA
    return pl.pallas_call(
        kernel,
        out_shape=jax.ShapeDtypeStruct((BLOCK, COLS), jnp.float32),
        in_specs=[pl.BlockSpec(memory_space=pltpu.VMEM)],
        out_specs=pl.BlockSpec(memory_space=pltpu.VMEM),
        scratch_shapes=[
            pltpu.VMEM((2, 32, BLOCK, 256), jnp.bfloat16),
            pltpu.VMEM((9, HALF, WIDE), jnp.float32),
            pltpu.VMEM((8, HALF, WIDE), jnp.float32),
            pltpu.VMEM((HALF, WIDE), jnp.float32),
            pltpu.VMEM((NZ // 2, HALF, WIDE), jnp.bfloat16),
            pltpu.VMEM((32, 2, HALF, WIDE), jnp.bfloat16),
            pltpu.VMEM((NZ, HALF, WIDE), jnp.bfloat16),
            dma((7,)),
            dma((2, 21)),
            dma((2, 9, SUBS)),
            dma((2, 5, PIECES)),
            dma((2, 22)),
            dma((2, 9, PIECES)),
        ],
        compiler_params=pltpu.CompilerParams(
            collective_id=0, has_side_effects=True, vmem_limit_bytes=48 * 1024 * 1024
        ),
        cost_estimate=pl.CostEstimate(
            flops=2300000000, bytes_accessed=700000, transcendentals=0
        ),
    )(iterate)


def solution(mesh):
    return jax.shard_map(
        local,
        mesh=mesh,
        in_specs=(P("row", "col"),),
        out_specs=P("row", "col"),
        check_vma=False,
    )
```

time: 151 us -> 131 us (0.87)
  Pallas kernels: 149 us -> 129 us
    pallas_call x1, Pallas kernels: 149 us -> 129 us  [local(): pl.pallas_call(kernel, out_shape=jax.ShapeDtypeStruct((BLOCK, COLS), jnp....]
where the time goes in v2:
time: 131 us
  Pallas kernels  129 us (98%)
  local copies, waits for them, and re-layouts  1.7 us (1%)
    pallas_call x1, Pallas kernels, local(): pl.pallas_call(kernel, out_shape=jax.ShapeDtypeStruct((BLOCK, COLS), jnp....  129 us

profile of v2, /device:TPU:6, one launch (start us, length us, event | category | flops | bytes accessed | tf_op | source)
XLA Modules:
  0.0 130.5 jit_solution(3548386328568424693)
XLA Ops:
  0.0 0.0 copy-start
  0.0 1.0 copy-done
  1.0 128.8 %shard_map.17 = f32[160,512]{1,0:T(8,128)S(1)} custom-call(f32[160,512]{1,0:T(8,128)S(1)} %copy-done), custom_call_target="tpu_custom_call" | custom-call | flops 2300000000 | bytes 700000 | tf_op jit(solution)/shard_map/pallas_call | solution.py:361
  129.8 0.7 copy.3
Async XLA Ops:
  0.0 1.0 copy-start

commit v3 on v2

v3 whole, which is shorter than its diff:
```python
import functools
import math

import jax
import jax.numpy as jnp
from jax import lax
from jax.experimental import pallas as pl
from jax.experimental.pallas import tpu as pltpu
from jax.sharding import PartitionSpec as P

coef_a = 3.4445
coef_b = -4.775
coef_c = 2.0315

NX = 4
NY = 4
NZ = 16
BLOCK = 160
HALF = 80
WIDE = 320
COLS = 512
CUT = 48
STRAIGHT = 8
LONG = 2 * (8 - STRAIGHT) + 1
PIECES = 5
MESH = pl.DeviceIdType.MESH


def remote(ref, send_sem, recv_sem, device):
    return pltpu.make_async_remote_copy(
        src_ref=ref,
        dst_ref=ref,
        send_sem=send_sem,
        recv_sem=recv_sem,
        device_id=device,
        device_id_type=MESH,
    )


class PlaneGather:
    def __init__(self, way, place, view, cut, total, send, recv):
        self.way, self.place, self.view = way, place, view
        self.cuts = ((0, cut), (cut, total - cut))
        self.send, self.recv = send, recv

    def coords(self, a, b):
        x, y, _, _ = self.place
        dx, dy = (a, b) if self.way == 0 else (b, a)
        return lax.rem(x + (dx % 4), 4), lax.rem(y + (dy % 4), 4)

    def block(self, a, b, core=None):
        x, y = self.coords(a, b)
        core = self.place[2] if core is None else core
        return core * 16 + y * 4 + x

    def device(self, a, b):
        x, y = self.coords(a, b)
        return {"row": (y * 4 + x) * 2 + self.place[2], "col": self.place[3]}

    def sibling(self):
        x, y, core, z = self.place
        return {"row": (y * 4 + x) * 2 + 1 - core, "col": z}

    def half(self, index, part):
        start, size = self.cuts[part]
        return self.view(index).at[pl.ds(start, size), :]

    def push(self, a, b, to, slot, part=None):
        index = self.block(a, b)
        ref = self.view(index) if part is None else self.half(index, part)
        device = self.sibling() if to is None else self.device(*to)
        remote(ref, self.send, self.recv.at[slot], device).start()

    def wait(self, a, b, slot, part=None, core=None):
        index = self.block(a, b, core)
        ref = self.view(index) if part is None else self.half(index, part)
        remote(ref, self.send, self.recv.at[slot], self.sibling()).wait_recv()

    def second(self, a):
        k = a % 4
        self.push(a, 0, (0, 1), 4 + 2 * k)
        self.push(a, 0, (0, -1), 5 + 2 * k)

    def other(self, a, b):
        self.push(a, b, None, 20)

    def own(self):
        self.push(0, 0, (1, 0), 0)
        self.push(0, 0, (-1, 0), 1)
        self.second(0)
        self.other(0, 0)

    def first(self):
        self.wait(-1, 0, 0)
        self.push(-1, 0, (1, 0), 2, part=0)
        self.second(-1)
        self.wait(1, 0, 1)
        self.push(1, 0, (-1, 0), 3, part=1)
        self.second(1)
        self.other(-1, 0)
        self.other(1, 0)

    def first_far(self):
        self.wait(2, 0, 2, part=0)
        self.wait(2, 0, 3, part=1)
        self.second(2)
        self.other(2, 0)

    def then(self, a):
        k = a % 4
        self.wait(a, -1, 4 + 2 * k)
        self.push(a, -1, (0, 1), 12 + 2 * k, part=0)
        self.wait(a, 1, 5 + 2 * k)
        self.push(a, 1, (0, -1), 13 + 2 * k, part=1)
        self.other(a, -1)
        self.other(a, 1)

    def then_far(self, a):
        k = a % 4
        self.wait(a, 2, 12 + 2 * k, part=0)
        self.wait(a, 2, 13 + 2 * k, part=1)
        self.other(a, 2)

    def others(self, blocks):
        remote(blocks, self.send, self.recv.at[20], self.sibling()).wait_recv()


STAGES = (
    lambda g: g.own(),
    lambda g: g.first(),
    lambda g: g.then(0),
    lambda g: g.first_far(),
    lambda g: g.then(-1),
    lambda g: g.then(1),
    lambda g: g.then_far(0),
    lambda g: g.then(2),
    lambda g: g.then_far(-1),
    lambda g: g.then_far(1),
    lambda g: g.then_far(2),
)


def fold(chunk):
    return jnp.concatenate([chunk[:HALF], chunk[HALF:]], axis=1)


class RingGather:
    def __init__(self, buf, place, stride, send, recv):
        self.buf, self.stride, self.send, self.recv = buf, stride, send, recv
        self.row, self.z = (place[1] * 4 + place[0]) * 2 + place[2], place[3]
        self.part = buf.shape[1] // PIECES
        self.far = NZ // stride // 2

    def plane(self, d):
        return lax.rem(self.z + d * self.stride + 2 * NZ, NZ)

    def copy(self, way, s, j):
        ref = self.buf.at[self.plane(1 - s if way == 0 else s - 1) // self.stride, pl.ds(j * self.part, self.part), :]
        device = {"row": self.row, "col": self.plane(1 if way == 0 else -1)}
        return remote(ref, self.send, self.recv.at[way, s, j], device)

    def wait(self, way, s, j):
        ref = self.buf.at[self.plane(-s if way == 0 else s) // self.stride, pl.ds(j * self.part, self.part), :]
        device = {"row": self.row, "col": self.plane(1)}
        remote(ref, self.send, self.recv.at[way, s, j], device).wait_recv()

    def pieces(self, last):
        for j in range(PIECES):
            for way in range(2):
                if not last or (way == 0) == (j < 3):
                    yield way, j

    def step(self, s, first=False, last=False):
        for way, j in self.pieces(last):
            if not first:
                self.wait(way, s - 1, j)
            self.copy(way, s, j).start()
        if last:
            for way, j in self.pieces(False):
                if (way == 0) != (j < 3):
                    self.wait(way, s - 1, j)

    def end(self):
        for way, j in self.pieces(True):
            self.wait(way, self.far, j)


def kernel(
    x_ref, out_ref,
    slab, xrow, xcol, gram, square, grow, gcol, mrow,
    sent, sr, xr, br, gr, cr, mr,
):
    row, z = lax.axis_index("row"), lax.axis_index("col")
    core = lax.rem(row, 2)
    x = lax.rem(row // 2, 4)
    y = row // 8
    place = (x, y, core, z)
    me = core * 16 + y * 4 + x
    up = {"row": row, "col": lax.rem(z + 1, NZ)}
    down = {"row": row, "col": lax.rem(z + NZ - 1, NZ)}

    def line(q):
        return q // 2

    def half(q):
        return pl.ds(pl.multiple_of(lax.rem(q, 2) * HALF, 16), HALF)

    gather_x = [
        PlaneGather(
            w, place, lambda i, w=w: slab.at[w, i], HALF, BLOCK, sent.at[0], sr.at[w]
        )
        for w in range(2)
    ]
    gather_c = [
        PlaneGather(
            w, place, lambda i, w=w: gcol.at[i, pl.ds(w * HALF, HALF), :], CUT, HALF, sent.at[8], cr.at[w]
        )
        for w in range(2)
    ]
    ring_x = RingGather(xrow, place, 1, sent.at[1], xr)
    ring_g = RingGather(grow, place, 1, sent.at[9], gr)
    ring_m = RingGather(mrow, place, 1, sent.at[10], mr)
    g0 = gather_x[0]
    east, west, north, south = g0.device(1, 0), g0.device(-1, 0), g0.device(0, 1), g0.device(0, -1)
    east2, north2 = g0.device(2, 0), g0.device(0, 2)
    sibling = g0.sibling()

    barrier = pltpu.get_barrier_semaphore()
    for device in (east, west, north, south, sibling, up, down):
        pl.semaphore_signal(barrier, inc=1, device_id=device, device_id_type=MESH)
    xrow[z] = x_ref[...].astype(jnp.bfloat16)
    slab[0, me] = x_ref[:, 0:256].astype(jnp.bfloat16)
    slab[1, me] = x_ref[:, 256:512].astype(jnp.bfloat16)
    gram[...] = jnp.zeros_like(gram)
    pl.semaphore_wait(barrier, 7)

    hands = core == line(z) // 4
    b = lax.rem(y + 4 - lax.rem(line(z), 4), 4)
    left, right = lax.rem(x + 3, 4), lax.rem(x + 1, 4)
    across = lax.rem(x + 2, 4)

    def whole(q, i):
        return xcol.at[q, i]

    def upper(q, i):
        return xcol.at[q, i, pl.ds(0, CUT), :]

    def lower(q, i):
        return xcol.at[q, i, pl.ds(CUT, HALF - CUT), :]

    def share(q, i):
        remote(whole(q, i), sent.at[7], br.at[q, 6], sibling).start()

    def spread(q, straight):
        @pl.when(straight)
        def _():
            remote(whole(q, x), sent.at[12], br.at[q, 4], east2).start()

        remote(whole(q, x), sent.at[4], br.at[q, 2], east).start()
        remote(whole(q, x), sent.at[5], br.at[q, 3], west).start()
        share(q, x)

    def source(q, straight):
        @pl.when(hands & (b == 0))
        def _():
            xcol[q, x] = xrow[q, half(z), :]

            @pl.when(straight)
            def _():
                remote(whole(q, x), sent.at[11], br.at[q, 0], north2).start()

            remote(whole(q, x), sent.at[2], br.at[q, 0], north).start()
            remote(whole(q, x), sent.at[3], br.at[q, 0], south).start()
            spread(q, straight)

    def relay(q, straight):
        @pl.when(hands & (lax.rem(b, 2) == 1))
        def _():
            remote(whole(q, x), sent.at[2], br.at[q, 0], north).wait_recv()

            @pl.when((b == 1) & jnp.logical_not(straight))
            def _():
                remote(upper(q, x), sent.at[2], br.at[q, 0], north).start()

            @pl.when((b == 3) & jnp.logical_not(straight))
            def _():
                remote(lower(q, x), sent.at[3], br.at[q, 1], south).start()

            spread(q, straight)

    def far(q, straight):
        @pl.when(hands & (b == 2))
        def _():
            @pl.when(straight)
            def _():
                remote(whole(q, x), sent.at[11], br.at[q, 0], north2).wait_recv()

            @pl.when(jnp.logical_not(straight))
            def _():
                remote(upper(q, x), sent.at[2], br.at[q, 0], north).wait_recv()
                remote(lower(q, x), sent.at[3], br.at[q, 1], south).wait_recv()

            spread(q, straight)

    def beside(q, straight):
        @pl.when(hands)
        def _():
            remote(whole(q, left), sent.at[4], br.at[q, 2], east).wait_recv()
            remote(whole(q, right), sent.at[5], br.at[q, 3], west).wait_recv()

            @pl.when(jnp.logical_not(straight))
            def _():
                remote(upper(q, left), sent.at[6], br.at[q, 4], east).start()
                remote(lower(q, right), sent.at[6], br.at[q, 5], west).start()

            share(q, left)
            share(q, right)

    def opposite(q, straight):
        @pl.when(hands)
        def _():
            @pl.when(straight)
            def _():
                remote(whole(q, across), sent.at[12], br.at[q, 4], east2).wait_recv()

            @pl.when(jnp.logical_not(straight))
            def _():
                remote(upper(q, across), sent.at[6], br.at[q, 4], east).wait_recv()
                remote(lower(q, across), sent.at[6], br.at[q, 5], west).wait_recv()

            share(q, across)

    def add(q, straight):
        @pl.when(jnp.logical_not(hands))
        def _():
            remote(xcol.at[q], sent.at[7], br.at[q, 6], sibling).wait_recv()

        gram[...] += lax.dot_general(
            xrow[q],
            xcol[q].reshape(WIDE, COLS),
            (((1,), (1,)), ((), ())),
            preferred_element_type=jnp.float32,
        )

    chain = (source, relay, far, beside, opposite, add)

    @pl.loop(0, NZ // 2 + len(chain))
    def _(t):
        @pl.when(t == 0)
        def _():
            ring_x.step(1, first=True)

        @pl.when((t > 0) & (t < 7))
        def _():
            ring_x.step(t + 1)

        @pl.when(t == 7)
        def _():
            ring_x.step(8, last=True)

        @pl.when(t == 8)
        def _():
            ring_x.end()

        for lag, action in enumerate(chain):
            n = t - lag

            @pl.when((n >= 0) & (n <= 8))
            def _(n=n, action=action):
                straight = n >= STRAIGHT
                action(lax.rem(z + n, NZ), straight)

                @pl.when((n > 0) & (n < 8))
                def _():
                    action(lax.rem(z + NZ - n, NZ), straight)

        for n, stage in enumerate(STAGES):

            @pl.when(t == n)
            def _(stage=stage):
                for g in gather_x:
                    stage(g)

    theirs = pl.ds((1 - core) * 16, 16)
    for g in gather_x:
        g.others(slab.at[g.way, theirs])

    gb = gram[...].astype(jnp.bfloat16)
    grow[z] = fold(gb)
    gcol[me] = gb
    square[...] = jnp.zeros_like(square)
    theirs = pl.ds((1 - core) * 16, 16)

    def unfold(ref, q):
        return jnp.concatenate([ref[q, :, 0:WIDE], ref[q, :, WIDE : 2 * WIDE]], axis=0)

    def square_step(d):
        q = lax.rem(z + d + NZ, NZ)
        square[...] += jnp.dot(
            unfold(grow, q),
            gcol[pl.ds(line(q) * 4, 4), half(q), :].reshape(WIDE, WIDE),
            preferred_element_type=jnp.float32,
        )

    ring_g.step(1, first=True)
    for s, stages in enumerate(((0,), (1,), (2, 3), (4, 5), (6, 7), (8, 9, 10)), 1):
        if s > 1:
            ring_g.step(s)
        for n in stages:
            for g in gather_c:
                STAGES[n](g)
    for w, g in enumerate(gather_c):
        g.others(gcol.at[theirs, pl.ds(w * HALF, HALF), :])

    @pl.loop(-2, 3)
    def _(d):
        square_step(d)

    ring_g.step(7)

    @pl.loop(3, 6)
    def _(d):
        square_step(d)
        square_step(-d)

    ring_g.step(8, last=True)
    for d in (6, -6, 7, -7):
        square_step(d)
    ring_g.end()
    square_step(8)

    mixed = (coef_b * gram[...] + coef_c * square[...]).astype(jnp.bfloat16)
    mrow[z] = fold(mixed)

    def product(d):
        q = lax.rem(z + d + NZ, NZ)
        left_rows = unfold(mrow, q)
        for h in range(2):
            out_ref[:, h * 256 : (h + 1) * 256] += jnp.dot(
                left_rows,
                slab[h, pl.ds(line(q) * 4, 4), half(q), :].reshape(WIDE, 256),
                preferred_element_type=jnp.float32,
            )

    ring_m.step(1, first=True)
    out_ref[...] = coef_a * x_ref[...]
    product(0)

    @pl.loop(2, 8)
    def _(s):
        ring_m.step(s)
        product(1 - s)
        product(s - 1)

    ring_m.step(8, last=True)
    product(-7)
    product(7)
    ring_m.end()
    product(8)
    out_ref[...] = (0.2 * math.sqrt(COLS * NZ)) * out_ref[...]

    def gone(k, ref):
        remote(ref, sent.at[k], sent.at[k], up).wait_send()

    gone(0, slab.at[:, pl.ds(0, 31)])
    gone(1, xrow.at[pl.ds(0, 15)])

    @pl.when(hands)
    def _():
        @pl.when(b == 0)
        def _():
            gone(2, xcol.at[:, 0])
            gone(3, xcol.at[:, 0])
            gone(11, xcol.at[pl.ds(0, LONG), 0])

        @pl.when(b == 1)
        def _():
            gone(2, xcol.at[pl.ds(0, NZ - LONG), 0, pl.ds(0, CUT), :])

        @pl.when(b == 3)
        def _():
            gone(3, xcol.at[pl.ds(0, NZ - LONG), 0, pl.ds(CUT, HALF - CUT), :])

        gone(4, xcol.at[:, 0])
        gone(5, xcol.at[:, 0])
        gone(6, xcol.at[pl.ds(0, NZ - LONG), 0])
        gone(7, xcol)
        gone(12, xcol.at[pl.ds(0, LONG), 0])

    gone(8, gcol.at[pl.ds(0, 31)])
    gone(9, grow.at[pl.ds(0, 15)])
    gone(10, mrow.at[pl.ds(0, 15)])


def local(iterate):
    dma = pltpu.SemaphoreType.DMA
    return pl.pallas_call(
        kernel,
        out_shape=jax.ShapeDtypeStruct((BLOCK, COLS), jnp.float32),
        in_specs=[pl.BlockSpec(memory_space=pltpu.VMEM)],
        out_specs=pl.BlockSpec(memory_space=pltpu.VMEM),
        scratch_shapes=[
            pltpu.VMEM((2, 32, BLOCK, 256), jnp.bfloat16),
            pltpu.VMEM((NZ, BLOCK, COLS), jnp.bfloat16),
            pltpu.VMEM((NZ, 4, HALF, COLS), jnp.bfloat16),
            pltpu.VMEM((BLOCK, WIDE), jnp.float32),
            pltpu.VMEM((BLOCK, WIDE), jnp.float32),
            pltpu.VMEM((NZ, HALF, 2 * WIDE), jnp.bfloat16),
            pltpu.VMEM((32, BLOCK, WIDE), jnp.bfloat16),
            pltpu.VMEM((NZ, HALF, 2 * WIDE), jnp.bfloat16),
            dma((13,)),
            dma((2, 21)),
            dma((2, 9, PIECES)),
            dma((NZ, 7)),
            dma((2, 9, PIECES)),
            dma((2, 21)),
            dma((2, 9, PIECES)),
        ],
        compiler_params=pltpu.CompilerParams(
            collective_id=0, has_side_effects=True, vmem_limit_bytes=48 * 1024 * 1024
        ),
        cost_estimate=pl.CostEstimate(
            flops=2300000000, bytes_accessed=700000, transcendentals=0
        ),
    )(iterate)


def solution(mesh):
    return jax.shard_map(
        local,
        mesh=mesh,
        in_specs=(P("row", "col"),),
        out_specs=P("row", "col"),
        check_vma=False,
    )
```

time: 131 us -> 124 us (0.947); the launches traced: 131 us -> 122 us
  Pallas kernels: 129 us -> 120 us
    pallas_call x1, Pallas kernels: 129 us -> 120 us  [local(): pl.pallas_call(kernel, out_shape=jax.ShapeDtypeStruct((BLOCK, COLS), jnp....]
where the time goes in v3:
time: 124 us; the launch traced here: 122 us
  Pallas kernels  120 us (97%)
  local copies, waits for them, and re-layouts  1.7 us (1%)
    pallas_call x1, Pallas kernels, local(): pl.pallas_call(kernel, out_shape=jax.ShapeDtypeStruct((BLOCK, COLS), jnp....  120 us

profile of v3, /device:TPU:6, one launch (start us, length us, event | category | flops | bytes accessed | tf_op | source)
XLA Modules:
  0.0 121.9 jit_solution(16476156724617813569)
XLA Ops:
  0.0 0.0 copy-start
  0.0 1.0 copy-done
  1.0 120.2 %shard_map.17 = f32[160,512]{1,0:T(8,128)S(1)} custom-call(f32[160,512]{1,0:T(8,128)S(1)} %copy-done), custom_call_target="tpu_custom_call" | custom-call | flops 2300000000 | bytes 700000 | tf_op jit(solution)/shard_map/pallas_call | solution.py:497
  121.2 0.7 copy.3
Async XLA Ops:
  0.0 1.0 copy-start

commit v4 on v3

--- a/solution.py
+++ b/solution.py
@@ -23,6 +23,7 @@
 STRAIGHT = 8
 LONG = 2 * (8 - STRAIGHT) + 1
 PIECES = 5
+SLOTS = 4
 MESH = pl.DeviceIdType.MESH
 
 
@@ -145,50 +146,53 @@
 
 
 class RingGather:
-    def __init__(self, buf, place, stride, send, recv):
-        self.buf, self.stride, self.send, self.recv = buf, stride, send, recv
+    def __init__(self, buf, place, pieces, send, recv):
+        self.buf, self.pieces, self.send, self.recv = buf, pieces, send, recv
         self.row, self.z = (place[1] * 4 + place[0]) * 2 + place[2], place[3]
-        self.part = buf.shape[1] // PIECES
-        self.far = NZ // stride // 2
+        self.part = buf.shape[1] // pieces
+        self.shared = (pieces + 1) // 2
 
     def plane(self, d):
-        return lax.rem(self.z + d * self.stride + 2 * NZ, NZ)
+        return lax.rem(self.z + d + 2 * NZ, NZ)
 
     def copy(self, way, s, j):
-        ref = self.buf.at[self.plane(1 - s if way == 0 else s - 1) // self.stride, pl.ds(j * self.part, self.part), :]
+        ref = self.piece(1 - s if way == 0 else s - 1, j)
         device = {"row": self.row, "col": self.plane(1 if way == 0 else -1)}
-        return remote(ref, self.send, self.recv.at[way, s, j], device)
+        return remote(ref, self.send, self.recv.at[way, s % SLOTS if isinstance(s, int) else lax.rem(s, SLOTS), j], device)
 
     def wait(self, way, s, j):
-        ref = self.buf.at[self.plane(-s if way == 0 else s) // self.stride, pl.ds(j * self.part, self.part), :]
+        ref = self.piece(-s if way == 0 else s, j)
         device = {"row": self.row, "col": self.plane(1)}
-        remote(ref, self.send, self.recv.at[way, s, j], device).wait_recv()
-
-    def pieces(self, last):
-        for j in range(PIECES):
+        remote(ref, self.send, self.recv.at[way, s % SLOTS if isinstance(s, int) else lax.rem(s, SLOTS), j], device).wait_recv()
+
+    def piece(self, d, j):
+        return self.buf.at[self.plane(d), pl.ds(pl.multiple_of(j * self.part, 16), self.part), :]
+
+    def step(self, s, first=False, last=False):
+        @pl.loop(0, self.pieces)
+        def _(j):
             for way in range(2):
-                if not last or (way == 0) == (j < 3):
-                    yield way, j
-
-    def step(self, s, first=False, last=False):
-        for way, j in self.pieces(last):
-            if not first:
-                self.wait(way, s - 1, j)
-            self.copy(way, s, j).start()
-        if last:
-            for way, j in self.pieces(False):
-                if (way == 0) != (j < 3):
+                if not first:
                     self.wait(way, s - 1, j)
+                if last:
+                    pl.when((j < self.shared) == (way == 0))(self.copy(way, s, j).start)
+                else:
+                    self.copy(way, s, j).start()
 
     def end(self):
-        for way, j in self.pieces(True):
-            self.wait(way, self.far, j)
+        @pl.loop(0, self.shared)
+        def _(j):
+            self.wait(0, NZ // 2, j)
+
+        @pl.loop(self.shared, self.pieces)
+        def _(j):
+            self.wait(1, NZ // 2, j)
 
 
 def kernel(
     x_ref, out_ref,
     slab, xrow, xcol, gram, square, grow, gcol, mrow,
-    sent, sr, xr, br, gr, cr, mr,
+    sent, sr, xr, br, gr, cr,
 ):
     row, z = lax.axis_index("row"), lax.axis_index("col")
     core = lax.rem(row, 2)
@@ -217,9 +221,9 @@
         )
         for w in range(2)
     ]
-    ring_x = RingGather(xrow, place, 1, sent.at[1], xr)
-    ring_g = RingGather(grow, place, 1, sent.at[9], gr)
-    ring_m = RingGather(mrow, place, 1, sent.at[10], mr)
+    ring_x = RingGather(xrow, place, PIECES, sent.at[1], xr)
+    ring_g = RingGather(grow, place, PIECES, sent.at[9], gr)
+    ring_m = RingGather(mrow, place, PIECES, sent.at[10], xr)
     g0 = gather_x[0]
     east, west, north, south = g0.device(1, 0), g0.device(-1, 0), g0.device(0, 1), g0.device(0, -1)
     east2, north2 = g0.device(2, 0), g0.device(0, 2)
@@ -249,15 +253,15 @@
         return xcol.at[q, i, pl.ds(CUT, HALF - CUT), :]
 
     def share(q, i):
-        remote(whole(q, i), sent.at[7], br.at[q, 6], sibling).start()
+        remote(whole(q, i), sent.at[7], br.at[q, 4], sibling).start()
 
     def spread(q, straight):
         @pl.when(straight)
         def _():
-            remote(whole(q, x), sent.at[12], br.at[q, 4], east2).start()
-
-        remote(whole(q, x), sent.at[4], br.at[q, 2], east).start()
-        remote(whole(q, x), sent.at[5], br.at[q, 3], west).start()
+            remote(whole(q, x), sent.at[12], br.at[q, 3], east2).start()
+
+        remote(whole(q, x), sent.at[4], br.at[q, 1], east).start()
+        remote(whole(q, x), sent.at[5], br.at[q, 2], west).start()
         share(q, x)
 
     def source(q, straight):
@@ -284,34 +288,26 @@
 
             @pl.when((b == 3) & jnp.logical_not(straight))
             def _():
-                remote(lower(q, x), sent.at[3], br.at[q, 1], south).start()
+                remote(lower(q, x), sent.at[3], br.at[q, 0], south).start()
 
             spread(q, straight)
 
     def far(q, straight):
         @pl.when(hands & (b == 2))
         def _():
-            @pl.when(straight)
-            def _():
-                remote(whole(q, x), sent.at[11], br.at[q, 0], north2).wait_recv()
+            remote(whole(q, x), sent.at[2], br.at[q, 0], north).wait_recv()
+            spread(q, straight)
+
+    def beside(q, straight):
+        @pl.when(hands)
+        def _():
+            remote(whole(q, left), sent.at[4], br.at[q, 1], east).wait_recv()
+            remote(whole(q, right), sent.at[5], br.at[q, 2], west).wait_recv()
 
             @pl.when(jnp.logical_not(straight))
             def _():
-                remote(upper(q, x), sent.at[2], br.at[q, 0], north).wait_recv()
-                remote(lower(q, x), sent.at[3], br.at[q, 1], south).wait_recv()
-
-            spread(q, straight)
-
-    def beside(q, straight):
-        @pl.when(hands)
-        def _():
-            remote(whole(q, left), sent.at[4], br.at[q, 2], east).wait_recv()
-            remote(whole(q, right), sent.at[5], br.at[q, 3], west).wait_recv()
-
-            @pl.when(jnp.logical_not(straight))
-            def _():
-                remote(upper(q, left), sent.at[6], br.at[q, 4], east).start()
-                remote(lower(q, right), sent.at[6], br.at[q, 5], west).start()
+                remote(upper(q, left), sent.at[6], br.at[q, 3], east).start()
+                remote(lower(q, right), sent.at[6], br.at[q, 3], west).start()
 
             share(q, left)
             share(q, right)
@@ -319,21 +315,13 @@
     def opposite(q, straight):
         @pl.when(hands)
         def _():
-            @pl.when(straight)
-            def _():
-                remote(whole(q, across), sent.at[12], br.at[q, 4], east2).wait_recv()
-
-            @pl.when(jnp.logical_not(straight))
-            def _():
-                remote(upper(q, across), sent.at[6], br.at[q, 4], east).wait_recv()
-                remote(lower(q, across), sent.at[6], br.at[q, 5], west).wait_recv()
-
+            remote(whole(q, across), sent.at[6], br.at[q, 3], east).wait_recv()
             share(q, across)
 
     def add(q, straight):
         @pl.when(jnp.logical_not(hands))
         def _():
-            remote(xcol.at[q], sent.at[7], br.at[q, 6], sibling).wait_recv()
+            remote(xcol.at[q], sent.at[7], br.at[q, 4], sibling).wait_recv()
 
         gram[...] += lax.dot_general(
             xrow[q],
@@ -365,14 +353,11 @@
         for lag, action in enumerate(chain):
             n = t - lag
 
-            @pl.when((n >= 0) & (n <= 8))
-            def _(n=n, action=action):
-                straight = n >= STRAIGHT
-                action(lax.rem(z + n, NZ), straight)
-
-                @pl.when((n > 0) & (n < 8))
-                def _():
-                    action(lax.rem(z + NZ - n, NZ), straight)
+            both = (n > 0) & (n < 8)
+
+            @pl.loop(0, jnp.where((n >= 0) & (n <= 8), jnp.where(both, 2, 1), 0))
+            def _(side, n=n, action=action):
+                action(lax.rem(z + jnp.where(side == 0, n, NZ - n), NZ), n >= STRAIGHT)
 
         for n, stage in enumerate(STAGES):
 
@@ -510,11 +495,10 @@
             pltpu.VMEM((NZ, HALF, 2 * WIDE), jnp.bfloat16),
             dma((13,)),
             dma((2, 21)),
-            dma((2, 9, PIECES)),
-            dma((NZ, 7)),
-            dma((2, 9, PIECES)),
+            dma((2, SLOTS, PIECES)),
+            dma((NZ, 5)),
+            dma((2, SLOTS, PIECES)),
             dma((2, 21)),
-            dma((2, 9, PIECES)),
         ],
         compiler_params=pltpu.CompilerParams(
             collective_id=0, has_side_effects=True, vmem_limit_bytes=48 * 1024 * 1024

time: 124 us -> 123 us (level)
    pallas_call x1, Pallas kernels: 120 us -> 119 us  [local(): pl.pallas_call(kernel, out_shape=jax.ShapeDtypeStruct((BLOCK, COLS), jnp....]
where the time goes in v4:
time: 123 us; the launch traced here: 121 us
  Pallas kernels  119 us (97%)
  local copies, waits for them, and re-layouts  1.7 us (1%)
    pallas_call x1, Pallas kernels, local(): pl.pallas_call(kernel, out_shape=jax.ShapeDtypeStruct((BLOCK, COLS), jnp....  119 us

profile of v4, /device:TPU:6, one launch (start us, length us, event | category | flops | bytes accessed | tf_op | source)
XLA Modules:
  0.0 120.6 jit_solution(370772117398651344)
XLA Ops:
  0.0 0.0 copy-start
  0.0 1.0 copy-done
  1.0 118.9 %shard_map.17 = f32[160,512]{1,0:T(8,128)S(1)} custom-call(f32[160,512]{1,0:T(8,128)S(1)} %copy-done), custom_call_target="tpu_custom_call" | custom-call | flops 2300000000 | bytes 700000 | tf_op jit(solution)/shard_map/pallas_call | solution.py:482
  119.8 0.7 copy.3
Async XLA Ops:
  0.0 1.0 copy-start

commit v5 on v4

--- a/solution.py
+++ b/solution.py
@@ -139,6 +139,10 @@
     lambda g: g.then_far(1),
     lambda g: g.then_far(2),
 )
+
+
+SLAB = 8
+WHEN = ((0,), (1,), (2,), (3, 4, 5), (6, 7), (8, 9, 10))
 
 
 def fold(chunk):
@@ -359,16 +363,12 @@
             def _(side, n=n, action=action):
                 action(lax.rem(z + jnp.where(side == 0, n, NZ - n), NZ), n >= STRAIGHT)
 
-        for n, stage in enumerate(STAGES):
+        for n, stage in enumerate(STAGES[:SLAB]):
 
             @pl.when(t == n)
             def _(stage=stage):
                 for g in gather_x:
                     stage(g)
-
-    theirs = pl.ds((1 - core) * 16, 16)
-    for g in gather_x:
-        g.others(slab.at[g.way, theirs])
 
     gb = gram[...].astype(jnp.bfloat16)
     grow[z] = fold(gb)
@@ -388,12 +388,17 @@
         )
 
     ring_g.step(1, first=True)
-    for s, stages in enumerate(((0,), (1,), (2, 3), (4, 5), (6, 7), (8, 9, 10)), 1):
+    for s, stages in enumerate(WHEN, 1):
         if s > 1:
             ring_g.step(s)
         for n in stages:
             for g in gather_c:
                 STAGES[n](g)
+        if s == 2:
+            for stage in STAGES[SLAB:]:
+                for g in gather_x:
+                    stage(g)
+    ring_g.step(7)
     for w, g in enumerate(gather_c):
         g.others(gcol.at[theirs, pl.ds(w * HALF, HALF), :])
 
@@ -401,16 +406,13 @@
     def _(d):
         square_step(d)
 
-    ring_g.step(7)
-
-    @pl.loop(3, 6)
+    ring_g.step(8, last=True)
+
+    @pl.loop(3, 8)
     def _(d):
         square_step(d)
         square_step(-d)
 
-    ring_g.step(8, last=True)
-    for d in (6, -6, 7, -7):
-        square_step(d)
     ring_g.end()
     square_step(8)
 
@@ -428,6 +430,8 @@
             )
 
     ring_m.step(1, first=True)
+    for g in gather_x:
+        g.others(slab.at[g.way, theirs])
     out_ref[...] = coef_a * x_ref[...]
     product(0)
 

time: 123 us -> 121 us (0.984)
  the two profiles are of different devices: /device:TPU:6 before, /device:TPU:40 now
where the time goes in v5:
time: 121 us
  Pallas kernels  119 us (98%)
  local copies, waits for them, and re-layouts  1.7 us (1%)
    pallas_call x1, Pallas kernels, local(): pl.pallas_call(kernel, out_shape=jax.ShapeDtypeStruct((BLOCK, COLS), jnp....  119 us

profile of v5, /device:TPU:40, one launch (start us, length us, event | category | flops | bytes accessed | tf_op | source)
XLA Modules:
  0.0 120.7 jit_solution(7081561658824060125)
XLA Ops:
  0.0 0.0 copy-start
  0.0 1.0 copy-done
  1.0 119.0 %shard_map.17 = f32[160,512]{1,0:T(8,128)S(1)} custom-call(f32[160,512]{1,0:T(8,128)S(1)} %copy-done), custom_call_target="tpu_custom_call" | custom-call | flops 2300000000 | bytes 700000 | tf_op jit(solution)/shard_map/pallas_call | solution.py:486
  119.9 0.7 copy.3
Async XLA Ops:
  0.0 1.0 copy-start

commit v6 on v5

--- a/solution.py
+++ b/solution.py
@@ -141,7 +141,7 @@
 )
 
 
-SLAB = 8
+SLAB = 9
 WHEN = ((0,), (1,), (2,), (3, 4, 5), (6, 7), (8, 9, 10))
 
 

time: 121 us -> 121 us (level)
  the two profiles are of different devices: /device:TPU:40 before, /device:TPU:6 now
where the time goes in v6:
time: 121 us; the launch traced here: 119 us
  Pallas kernels  117 us (97%)
  local copies, waits for them, and re-layouts  1.7 us (1%)
    pallas_call x1, Pallas kernels, local(): pl.pallas_call(kernel, out_shape=jax.ShapeDtypeStruct((BLOCK, COLS), jnp....  117 us

profile of v6, /device:TPU:6, one launch (start us, length us, event | category | flops | bytes accessed | tf_op | source)
XLA Modules:
  0.0 118.5 jit_solution(11065217568125263922)
XLA Ops:
  0.0 0.0 copy-start
  0.0 1.0 copy-done
  1.0 116.8 %shard_map.17 = f32[160,512]{1,0:T(8,128)S(1)} custom-call(f32[160,512]{1,0:T(8,128)S(1)} %copy-done), custom_call_target="tpu_custom_call" | custom-call | flops 2300000000 | bytes 700000 | tf_op jit(solution)/shard_map/pallas_call | solution.py:486
  117.8 0.7 copy.3
Async XLA Ops:
  0.0 1.0 copy-start
